TPU v7x, 512 devices: a whole 4x4x16 slice. The times are simulated.
512 devices in a mesh: pair: 128 (over x, y_lo, z), view: 2 (over y_hi), head: 2 (over core).
Axes of the slice: x: 4, y: 4 (y_hi: 2, y_lo: 2; y = y_hi * 2 + y_lo), z: 16, core: 2. Of those that a mesh axis runs over, the one named last changes fastest.
Arguments:
- enc_tokens: bfloat16 [128, 512, 1024], P('pair', ('view', 'head')), may hold values from -6 to 6
- pairs: int32 [128, 2], replicated, may hold values from 0 to 127, all different within a row
- image_slot: int32 [128], replicated, may hold values from 0 to 127, each once
- embed_weight: bfloat16 [1024, 768], replicated, may hold values from -0.1875 to 0.1875
- norm_gains: float32 [2, 2, 768], P('view'), may hold values from 0.5 to 1.5
- cross_q: bfloat16 [2, 768, 768], P('view', None, 'head'), may hold values from -1 to 1
- cross_kv: bfloat16 [2, 768, 2, 768], P('view', None, None, 'head'), may hold values from -4 to 4
- cross_out: bfloat16 [2, 768, 768], P('view', None, 'head'), may hold values from -0.21875 to 0.21875
Outputs:
- joined: bfloat16 [128, 512, 768], P('pair', ('view', 'head'))
Inputs may be any that keep to these rules, and one draw needn't show every extreme that they name: `pairs`: each row names two different images, and every image is named by some row. `image_slot`: each image has its own slot.
All inputs are finite; a program needn't handle non-finite values.
Results may differ from a plain program's by a relative error of at most 0.0064.
Values may be sent and summed in bfloat16 or wider, within the bound.
A program may use at most 64 MiB of HBM per device.

v0:
```python
import jax
import jax.numpy as jnp
from jax import lax
from jax.sharding import PartitionSpec as P

HD = 64
GRIDW = 32


def normalize(inputs, gain):
    inputs = inputs.astype(jnp.float32)
    centered = inputs - jnp.mean(inputs, axis=-1, keepdims=True)
    variance = jnp.mean(centered * centered, axis=-1, keepdims=True)
    return (centered * lax.rsqrt(variance + 1e-06) * gain).astype(jnp.bfloat16)


def rotate(inputs, head_dim, grid_width):
    token_count = inputs.shape[0]
    half_dim = head_dim // 2
    quarter_dim = half_dim // 2
    split_up = inputs.reshape(token_count, -1, 2, 2, quarter_dim)
    row_index = jnp.arange(token_count, dtype=jnp.int32)
    places = jnp.stack([row_index // grid_width, row_index % grid_width], axis=1).astype(
        jnp.float32
    )
    frequency = 100.0 ** (-2.0 * jnp.arange(quarter_dim, dtype=jnp.float32) / half_dim)
    angles = places[:, None, :, None] * frequency
    cosine = jnp.cos(angles)
    sine_table = jnp.sin(angles)
    first_part = split_up[:, :, :, 0, :]
    second_part = split_up[:, :, :, 1, :]
    turned = jnp.stack(
        [
            first_part * cosine - second_part * sine_table,
            second_part * cosine + first_part * sine_table,
        ],
        axis=3,
    )
    return turned.reshape(inputs.shape)


def attend(queries, key_rows, value_rows, head_dim):
    token_count = queries.shape[0]
    query_heads = queries.reshape(token_count, -1, head_dim).transpose(1, 0, 2)
    key_heads = key_rows.reshape(key_rows.shape[0], -1, head_dim).transpose(1, 0, 2)
    value_heads = value_rows.reshape(value_rows.shape[0], -1, head_dim).transpose(1, 0, 2)
    scale = head_dim ** (-0.5)

    def one_head(members):
        query_block, key_block, value_block = members
        scores = (
            lax.dot_general(
                query_block, key_block, (((1,), (1,)), ((), ())), preferred_element_type=jnp.float32
            )
            * scale
        )
        row_top = jnp.max(scores, axis=-1, keepdims=True)
        expo = jnp.exp(scores - row_top)
        row_total = jnp.sum(expo, axis=-1, keepdims=True)
        weights = (expo / row_total).astype(jnp.bfloat16)
        return jnp.dot(weights, value_block, preferred_element_type=jnp.float32).astype(
            jnp.bfloat16
        )

    attended = lax.map(one_head, (query_heads, key_heads, value_heads))
    return attended.transpose(1, 0, 2).reshape(token_count, -1)


def embed_rows(weight, token_block):
    flattened = token_block.reshape(-1, token_block.shape[-1])
    embedded = jnp.dot(flattened, weight, preferred_element_type=jnp.float32)
    return embedded.astype(jnp.bfloat16).reshape(token_block.shape[:-1] + (weight.shape[1],))


def body(enc_tokens, pairs, image_slot, embed_weight, norm_gains, cross_q, cross_kv, cross_out):
    holders = lax.axis_size("pair")
    groups = lax.axis_size("view") * lax.axis_size("head")
    quarter_rows = enc_tokens.shape[1]
    per_holder = quarter_rows // holders
    model_width = embed_weight.shape[1]
    holdings = lax.all_to_all(enc_tokens, "pair", split_axis=1, concat_axis=0, tiled=True)
    slot_pairs = image_slot[pairs]
    outgoing = jnp.take(holdings, slot_pairs.T, axis=0)
    arrived = embed_rows(
        embed_weight, lax.all_to_all(outgoing, "pair", split_axis=1, concat_axis=1, tiled=True)
    )
    own_quarter = arrived.reshape(2, quarter_rows, model_width)
    pair_tokens = lax.all_gather(own_quarter, ("view", "head"), axis=1, tiled=True)
    branch_index = lax.axis_index("view")
    own_tokens = lax.dynamic_index_in_dim(pair_tokens, branch_index, 0, keepdims=False)
    partner = lax.dynamic_index_in_dim(pair_tokens, 1 - branch_index, 0, keepdims=False)
    branch_gains = norm_gains[0]
    query_in = normalize(own_tokens, branch_gains[0])
    key_in = normalize(partner, branch_gains[1])
    queries = rotate(
        jnp.dot(query_in, cross_q[0], preferred_element_type=jnp.float32), HD, GRIDW
    ).astype(jnp.bfloat16)
    projected = jnp.einsum("td,dch->tch", key_in, cross_kv[0], preferred_element_type=jnp.float32)
    key_rows = rotate(projected[:, 0], HD, GRIDW).astype(jnp.bfloat16)
    value_rows = projected[:, 1].astype(jnp.bfloat16)
    attended = attend(queries, key_rows, value_rows, HD)
    partial_sum = lax.dot_general(
        attended, cross_out[0], (((1,), (1,)), ((), ())), preferred_element_type=jnp.float32
    )
    first_head = (lax.axis_index("head") == 0).astype(jnp.float32)
    partial_sum = partial_sum + first_head * own_tokens.astype(jnp.float32)
    stacked = partial_sum.reshape(groups, holders, per_holder, model_width)
    returned = lax.all_to_all(stacked, "pair", split_axis=1, concat_axis=1, tiled=True)
    branch_slots = lax.dynamic_index_in_dim(slot_pairs, branch_index, 1, keepdims=False)
    slot_table = (jnp.arange(holders, dtype=jnp.int32)[:, None] == branch_slots[None, :]).astype(
        jnp.float32
    )
    summed = jnp.einsum("sq,kqjd->ksjd", slot_table, returned, precision=lax.Precision.HIGHEST)
    combined = lax.psum_scatter(summed, ("view", "head"), scatter_dimension=0, tiled=True)
    use_count = jnp.sum(
        (slot_pairs.reshape(-1)[None, :] == jnp.arange(holders, dtype=jnp.int32)[:, None]).astype(
            jnp.float32
        ),
        axis=1,
    )
    average = (combined / use_count[None, :, None, None]).astype(jnp.bfloat16)
    landed = lax.all_to_all(average, "pair", split_axis=1, concat_axis=2, tiled=True)
    return landed.reshape(1, quarter_rows, model_width)


def solution(mesh):
    placed = (
        P("pair", ("view", "head"), None),
        P(),
        P(),
        P(),
        P("view", None, None),
        P("view", None, "head"),
        P("view", None, None, "head"),
        P("view", None, "head"),
    )
    return jax.shard_map(
        body,
        mesh=mesh,
        in_specs=placed,
        out_specs=P("pair", ("view", "head"), None),
        check_vma=False,
    )
```

profile of v0, /device:TPU:1, one launch (start us, length us, event | category | flops | bytes accessed | tf_op | source)
XLA Modules:
  0.0 344.3 jit_solution(13944974693177656157)
XLA Ops:
  6.5 1.5 copy.84
  8.0 0.5 broadcast.247
  8.5 2.3 reduce.8
  10.8 0.9 reshape.243
  11.6 21.3 %all-to-all-start = ((bf16[128,2,512]{2,1,0:T(2,128)(2,1)}), bf16[128,2,512]{2,1,0:T(2,128)(2,1)S(1)}, u32[]{:S(2)}, u32[]{:S(2)}) async-start(bf16[128,2,512]{2,1,0:T(2,128)(2,1)} %reshape.243), calls=%async_computation | async-start | bytes 524288 | tf_op jit(solution)/shard_map/all_to_all | solution.py:81
  33.1 0.1 copy.60
  33.2 0.1 reshape.214
  33.3 1.9 gather_fusion
  35.2 0.1 reshape.213
  35.5 18.3 %all-to-all-done = bf16[128,2,512]{2,1,0:T(2,128)(2,1)S(1)} async-done(((bf16[128,2,512]{2,1,0:T(2,128)(2,1)}), bf16[128,2,512]{2,1,0:T(2,128)(2,1)S(1)}, u32[]{:S(2)}, u32[]{:S(2)}) %all-to-all-start) | async-done | bytes 262176 | tf_op jit(solution)/shard_map/all_to_all | solution.py:81
  53.8 0.2 reshape.244
  54.1 0.1 copy.82
  54.2 1.2 gather_fusion.1
  55.3 0.7 broadcast_select_fusion
  56.0 36.7 %all_to_all.31 = bf16[2,128,1,1024]{3,0,2,1:T(2,128)(2,1)S(1)} all-to-all(bf16[2,128,1,1024]{3,0,2,1:T(2,128)(2,1)S(1)} %broadcast_select_fusion), channel_id=1, replica_groups=mesh['pair'=128,'view'=2,'head'=2] {'pair'}, dimensions={1} | all-to-all | bytes 1048576 | tf_op jit(solution)/shard_map/all_to_all | solution.py:85
  92.8 0.1 copy.64
  92.9 1.4 convolution_convert_fusion.1
  94.4 1.1 copy.65
  95.5 0.9 multiply_cosine_fusion
  96.4 25.3 %all-gather.2.cloned.1.call-done = bf16[2,512,768]{2,1,0:T(8,128)(2,1)} async-done(((bf16[2,128,768]{2,1,0:T(8,128)(2,1)}), bf16[2,512,768]{2,1,0:T(8,128)(2,1)}) %all-gather.2.cloned.1.call-update) | async-done | bytes 1572880 | tf_op jit(solution)/shard_map/all_gather | solution.py:88
  121.8 1.8 convert_reduce_fusion
  123.6 0.6 fusion.24
  124.3 1.0 fusion.30
  125.3 1.0 slice.41
  126.3 1.2 copy.69
  127.5 1.8 fusion.35
  129.3 1.0 subtract_convert_fusion
  130.4 1.2 copy.68
  131.6 1.1 pad_maximum_fusion
  132.6 1.2 copy.66
  133.8 19.9 %while.10 = (s32[]{:T(128)}, bf16[6,512,64]{1,2,0:T(8,128)(2,1)}, bf16[6,512,64]{2,1,0:T(8,128)(2,1)}, bf16[6,512,64]{2,1,0:T(8,128)(2,1)}, bf16[6,512,64]{2,1,0:T(8,128)(2,1)}, /*index=5*/s32[]{:T(128)}) while((s32[]{:T(128)}, bf16[6,512,64]{1,2,0:T(8,128)(2,1)}, bf16[6,512,64]{2,1,0:T(8,128)(2,1)}, bf16[6,512,64]{2,1,0:T(8,128)(2,1)}, ...), condition=%wide.region_7.8_spmd, body=%wide.region_4.7_spmd.sunk | while | flops 68975616 | bytes 3616845 | solution.py:65
  133.8 1.3 fusion.61
  135.1 0.2 fusion.62
  135.3 1.8 fusion.63
  137.1 1.3 fusion.61
  138.4 0.2 fusion.62
  138.6 1.8 fusion.63
  140.4 1.3 fusion.61
  141.7 0.2 fusion.62
  141.9 1.8 fusion.63
  143.7 1.3 fusion.61
  145.0 0.2 fusion.62
  145.2 1.8 fusion.63
  147.0 1.3 fusion.61
  148.3 0.2 fusion.62
  148.5 1.8 fusion.63
  150.3 1.3 fusion.61
  151.6 0.2 fusion.62
  151.8 1.8 fusion.63
  153.6 1.8 fusion.15
  155.5 2.2 copy.70
  157.6 16.7 %all-to-all-start.2 = ((f32[4,128,1,768]{3,0,2,1:T(4,128)}), f32[4,128,1,768]{3,0,2,1:T(4,128)S(1)}, u32[]{:S(2)}, u32[]{:S(2)}) async-start(f32[4,128,1,768]{3,0,2,1:T(4,128)} %copy.70), calls=%async_computation.2 | async-start | bytes 3145728 | tf_op jit(solution)/shard_map/all_to_all | solution.py:108
  174.4 0.2 dynamic-slice_reduce_fusion
  174.6 69.0 %all-to-all-done.2 = f32[4,128,1,768]{3,0,2,1:T(4,128)S(1)} async-done(((f32[4,128,1,768]{3,0,2,1:T(4,128)}), f32[4,128,1,768]{3,0,2,1:T(4,128)S(1)}, u32[]{:S(2)}, u32[]{:S(2)}) %all-to-all-start.2) | async-done | bytes 1572896 | tf_op jit(solution)/shard_map/all_to_all | solution.py:108
  243.6 1.6 copy.71
  245.2 3.4 fusion.27
  248.6 0.1 convert_reduce_fusion.2
  248.7 50.2 %reduce-scatter.2.cloned.1.call-done = f32[1,128,1,768]{1,3,0,2:T(8,128)} async-done(((f32[4,128,1,768]{1,3,0,2:T(8,128)}), f32[1,128,1,768]{1,3,0,2:T(8,128)}) %reduce-scatter.2.cloned.1.call-update) | async-done | bytes 393232 | tf_op jit(solution)/shard_map/reduce_scatter | solution.py:114
  298.9 1.0 divide_convert_fusion.2
  299.9 0.4 copy.72
  300.4 1.8 reduce.9
  302.2 34.5 %all_to_all.32 = bf16[128,2,384]{2,1,0:T(2,128)(2,1)S(1)} all-to-all(bf16[128,2,384]{2,1,0:T(2,128)(2,1)S(1)} %reshape.245), channel_id=1, replica_groups=mesh['pair'=128,'view'=2,'head'=2] {'pair'}, dimensions={0} | all-to-all | bytes 393216 | tf_op jit(solution)/shard_map/all_to_all | solution.py:122
  336.7 0.1 reshape.246
  336.8 0.7 copy.83
  (45 shorter events, 0.6 us)
Async XLA Ops:
  6.5 86.4 %copy-start = (bf16[1024,768]{1,0:T(8,128)(2,1)S(1)}, bf16[1024,768]{1,0:T(8,128)(2,1)}, u32[]{:S(2)}) copy-start(bf16[1024,768]{1,0:T(8,128)(2,1)} %param.13) | copy-start | bytes 4718596
  6.5 26.5 %copy-start.10 = (s32[128,2]{0,1:T(2,128)S(1)}, s32[128,2]{0,1:T(2,128)}, u32[]{:S(2)}) copy-start(s32[128,2]{0,1:T(2,128)} %param.11) | copy-start | bytes 3076
  6.5 26.8 %copy-start.1 = (s32[128]{0:T(128)S(1)}, s32[128]{0:T(128)}, u32[]{:S(2)}) copy-start(s32[128]{0:T(128)} %param.12) | copy-start | bytes 1540
  11.6 42.2 %all-to-all-start = ((bf16[128,2,512]{2,1,0:T(2,128)(2,1)}), bf16[128,2,512]{2,1,0:T(2,128)(2,1)S(1)}, u32[]{:S(2)}, u32[]{:S(2)}) async-start(bf16[128,2,512]{2,1,0:T(2,128)(2,1)} %reshape.243), calls=%async_computation | async-start | bytes 524288 | tf_op jit(solution)/shard_map/all_to_all | solution.py:81
  33.0 88.8 %all-gather.2.cloned.1.call-start = ((), (), s32[]{:S(2)}) async-start(), calls=%async_computation.5 | async-start | bytes 1966080 | tf_op jit(solution)/shard_map/all_gather | solution.py:88
  35.4 18.7 %copy-start.4 = (s32[128,2]{1,0:T(8,128)}, s32[128,2]{1,0:T(8,128)S(1)}, u32[]{:S(2)}) copy-start(s32[128,2]{1,0:T(8,128)S(1)} %reshape.213) | copy-start | bytes 3076
  92.9 1.4 copy-start.6
  92.9 2.5 copy-start.9
  121.8 1.9 copy-start.2
  121.8 2.5 copy-start.11
  127.5 1.8 copy-start.3
  127.5 1.8 copy-start.7
  127.5 1.8 copy-start.8
  157.6 16.8 %copy-start.5 = (s32[128,2]{1,0:T(8,128)S(1)}, s32[128,2]{1,0:T(8,128)}, u32[]{:S(2)}) copy-start(s32[128,2]{1,0:T(8,128)} %copy-done.4) | copy-start | bytes 3076
  157.6 85.9 %all-to-all-start.2 = ((f32[4,128,1,768]{3,0,2,1:T(4,128)}), f32[4,128,1,768]{3,0,2,1:T(4,128)S(1)}, u32[]{:S(2)}, u32[]{:S(2)}) async-start(f32[4,128,1,768]{3,0,2,1:T(4,128)} %copy.70), calls=%async_computation.2 | async-start | bytes 3145728 | tf_op jit(solution)/shard_map/all_to_all | solution.py:108
  174.3 124.6 %reduce-scatter.2.cloned.1.call-start = ((), (), s32[]{:S(2)}) async-start(), calls=%async_computation.6 | async-start | bytes 1966080 | tf_op jit(solution)/shard_map/reduce_scatter | solution.py:114
Sparse Core Ops, SparseCore 0:
  94.4 27.2 all-gather.1
  248.7 50.1 reduce-scatter.1
where the time goes:
time: 347 us; the launch traced here: 344 us
  waiting for transfers between devices  163 us (47%)
  blocking collectives  71.2 us (21%)
  starting transfers between devices  38.1 us (11%)
  matrix products  28 us (8%)
  local copies, waits for them, and re-layouts  17.8 us (5%)
  between operations  13.8 us (4%)
  other arithmetic  12.6 us (4%)
    all_to_all x1, waiting for transfers between devices, body(): lax.all_to_all(stacked, 'pair', split_axis=1, concat_axis=1, tiled=True)  69 us
    reduce_scatter x1, waiting for transfers between devices, body(): lax.psum_scatter(summed, ('view', 'head'), scatter_dimension=0, tiled=True)  50.2 us
    all_to_all x1, blocking collectives, body(): lax.all_to_all(outgoing, 'pair', split_axis=1, concat_axis=1, tiled=True)  36.7 us
    all_to_all x1, blocking collectives, body(): lax.all_to_all(average, 'pair', split_axis=1, concat_axis=2, tiled=True)  34.5 us
    all_gather x1, waiting for transfers between devices, body(): lax.all_gather(own_quarter, ('view', 'head'), axis=1, tiled=True)  25.3 us
    all_to_all x1, starting transfers between devices, body(): lax.all_to_all(enc_tokens, 'pair', split_axis=1, concat_axis=0, tiled=True)  21.3 us
    all_to_all x1, waiting for transfers between devices, body(): lax.all_to_all(enc_tokens, 'pair', split_axis=1, concat_axis=0, tiled=True)  18.3 us
    all_to_all x1, starting transfers between devices, body(): lax.all_to_all(stacked, 'pair', split_axis=1, concat_axis=1, tiled=True)  16.7 us
  transfers between devices with their start and end apart: 4, of which 4 were waited for; matrix products, arithmetic and copies ran while one was open for 1% of the time, Pallas kernels for 0%

commit v1 on v0

v1 whole, which is shorter than its diff:
```python
import jax
import jax.numpy as jnp
import numpy as np
from jax import lax
from jax.experimental import pallas as pl
from jax.experimental.pallas import tpu as pltpu
from jax.sharding import PartitionSpec as P

HD = 64
GRIDW = 32
TOK = 512
DD = 768
HALF = 384
NP = 128
BF = jnp.bfloat16
F32 = jnp.float32
MESH = pl.DeviceIdType.MESH


def rope_tables():
    lane = np.arange(128)
    token = np.arange(TOK)
    place = np.where(
        ((lane % HD) // 32)[None, :] == 0, (token // GRIDW)[:, None], (token % GRIDW)[:, None]
    ).astype(np.float64)
    frequency = 100.0 ** (-2.0 * (lane % 16) / 32.0)
    angle = place * frequency[None, :]
    sign = np.where((lane % 32) < 16, -1.0, 1.0)
    return np.cos(angle).astype(np.float32), (np.sin(angle) * sign[None, :]).astype(np.float32)


def iota(shape, dim):
    return lax.broadcasted_iota(jnp.int32, shape, dim)


def onehot(mask):
    return jnp.where(mask, 1.0, 0.0).astype(BF)


def dot(a, b, dims=((1,), (0,))):
    return lax.dot_general(a, b, (dims, ((), ())), preferred_element_type=F32)


def kernel(
    x_ref, pairs_ref, slot_ref, emb_ref, gain_ref, wq_ref, wkv_ref, wo_ref, cos_ref, sin_ref,
    out_ref,
    e_ref, s1, h_ref, s2, t_ref, f_ref, wk, wv, wox, qkv, att, attx, yb, yx, s3, r_ref, s4, z_ref,
    local_sem, wo_sem, p1, p2, ysem, csem, fsem, asem, bsem, p3, p4,
):
    me = lax.axis_index("pair")
    view = lax.axis_index("view")
    core = lax.axis_index("head")
    mine = view * 2 + core
    across = view * 2 + 1 - core
    to_core = {"head": 1 - core}
    to_view = {"view": 1 - view}

    def remote(src, dst, sems, where):
        return pltpu.make_async_remote_copy(
            src, dst, sems.at[0], sems.at[1], device_id=where, device_id_type=MESH
        )

    barrier = pltpu.get_barrier_semaphore()

    def greet(k, carry):
        pl.semaphore_signal(
            barrier, inc=1, device_id={"pair": lax.rem(me + k, NP)}, device_id_type=MESH
        )
        return carry

    pl.semaphore_signal(barrier, inc=1, device_id=to_core, device_id_type=MESH)
    pl.semaphore_signal(barrier, inc=1, device_id=to_view, device_id_type=MESH)
    lax.fori_loop(1, NP, greet, 0)

    def scatter(src, dst, sems):
        def send(k, carry):
            peer = lax.rem(me + k, NP)
            remote(src.at[peer], dst.at[me], sems, {"pair": peer}).start()
            return carry

        lax.fori_loop(1, NP, send, 0)

    def landed(buf, sem):
        whole = buf.at[pl.ds(0, NP - 1)]
        pltpu.make_async_copy(whole, whole, sem).wait()

    weave = [onehot(iota((2 * NP, NP), 0) == 2 * iota((2 * NP, NP), 1) + f) for f in range(2)]
    part = [onehot(iota((NP, 2 * NP), 1) == 2 * iota((NP, 2 * NP), 0) + f) for f in range(2)]

    def interleave(rows):
        mixed = dot(weave[0], rows[:, :HALF]) + dot(weave[1], rows[:, HALF:])
        return mixed.astype(BF).reshape(NP, 2, HALF)

    def separate(rows):
        flat = rows.reshape(2 * NP, HALF)
        return dot(part[0], flat), dot(part[1], flat)

    e_ref[...] = dot(x_ref[...], emb_ref[...]).astype(BF)
    s1[...] = interleave(e_ref[...])
    pl.semaphore_wait(barrier, NP + 1)
    scatter(s1, h_ref, p1)
    h_ref[me] = s1[me]
    remote(wo_ref, wox, wo_sem, to_core).start()

    pair_col = dot(
        onehot(iota((2 * NP, NP), 0) // 2 == iota((2 * NP, NP), 1)), pairs_ref[...].astype(BF)
    )
    slot_rows = onehot(iota((2 * NP, NP), 0) // 2 == slot_ref[...])
    same = (iota((2 * NP, 2 * NP), 0) - iota((2 * NP, 2 * NP), 1)) % 2 == 0
    pick, spread = [], []
    for b in range(2):
        image = onehot(iota((2 * NP, NP), 1) == pair_col[:, b : b + 1].astype(jnp.int32))
        pick.append(jnp.where(same, dot(image, slot_rows, ((1,), (1,))), 0.0).astype(BF))
        spread.append(jnp.where(same, dot(slot_rows, image, ((1,), (1,))), 0.0).astype(BF))
    uses = jnp.sum(spread[0].astype(F32) + spread[1].astype(F32), axis=1, keepdims=True)

    for block in range(DD // NP):
        first, second = separate(wkv_ref[block * NP : (block + 1) * NP])
        wk[block * NP : (block + 1) * NP, :] = first.astype(BF)
        wv[block * NP : (block + 1) * NP, :] = second.astype(BF)

    landed(h_ref, p1.at[1])
    held = h_ref[...].reshape(2 * NP, HALF)
    for b in range(2):
        s2[b] = dot(pick[b], held).astype(BF).reshape(NP, 2, HALF)
        scatter(s2.at[b], t_ref.at[b], p2.at[b])
        t_ref[b, me] = s2[b, me]

    for b in range(2):
        landed(t_ref.at[b], p2.at[b, 1])
        first, second = separate(t_ref[b])
        f_ref[b, mine, :, :HALF] = first.astype(BF)
        f_ref[b, mine, :, HALF:] = second.astype(BF)
        remote(f_ref.at[b, mine], f_ref.at[b, mine], ysem.at[b], to_view).start()
        remote(f_ref.at[b, mine], f_ref.at[b, mine], csem.at[b], to_core).start()
    there = (1 - view) * 2 + core
    for b in range(2):
        arrived = f_ref.at[b, there]
        pltpu.make_async_copy(arrived, arrived, ysem.at[b, 1]).wait()
        remote(arrived, arrived, fsem.at[b], to_core).start()
    for b in range(2):
        block = f_ref.at[b, mine]
        pltpu.make_async_copy(block, block, csem.at[b, 1]).wait()
        pltpu.make_async_copy(block, block, fsem.at[b, 1]).wait()

    def normalize(rows, gain):
        rows = rows.astype(F32)
        centered = rows - jnp.mean(rows, axis=-1, keepdims=True)
        variance = jnp.mean(centered * centered, axis=-1, keepdims=True)
        return (centered * lax.rsqrt(variance + 1e-06) * gain).astype(BF)

    low16 = iota((NP, 128), 1) % 32 < 16

    def rotate(rows, cosine, sine, scale):
        parts = []
        for block in range(HALF // 128):
            u = rows[:, block * 128 : (block + 1) * 128]
            swapped = jnp.where(low16, pltpu.roll(u, 112, 1), pltpu.roll(u, 16, 1))
            parts.append((u * cosine + swapped * sine).astype(BF) * scale)
        return jnp.concatenate(parts, axis=1)

    def project(quarter, carry):
        rows = pl.ds(pl.multiple_of(quarter * NP, NP), NP)
        cosine, sine = cos_ref[rows, :], sin_ref[rows, :]
        query_in = normalize(f_ref[view, quarter], gain_ref[0:1, :])
        qkv[0, rows, :] = rotate(dot(query_in, wq_ref[...]), cosine, sine, BF(HD**-0.5))
        key_in = normalize(f_ref[1 - view, quarter], gain_ref[1:2, :])
        qkv[1, rows, :] = rotate(dot(key_in, wk[...]), cosine, sine, BF(1.0))
        qkv[2, rows, :] = dot(key_in, wv[...]).astype(BF)
        return carry

    lax.fori_loop(0, 4, project, 0)

    wox_wait = remote(wo_ref, wox, wo_sem, to_core)
    wox_wait.wait_recv()

    left_q = iota((2 * NP, 128), 1) < HD
    left_k = iota((TOK, 128), 1) < HD
    one = jnp.ones((), BF)
    zero = jnp.zeros((), BF)
    for step in range(2):
        half = 1 - view if step == 0 else view
        rows = pl.ds(pl.multiple_of(half * 2 * NP, 2 * NP), 2 * NP)
        for block in range(HALF // 128):
            columns = slice(block * 128, (block + 1) * 128)
            queries = qkv[0, rows, columns]
            keys = qkv[1, :, columns]
            values = qkv[2, :, columns]
            results = []
            for side in range(2):
                own_q = left_q if side == 0 else jnp.logical_not(left_q)
                own_k = left_k if side == 0 else jnp.logical_not(left_k)
                scores = dot(jnp.where(own_q, queries, zero), keys, ((1,), (1,)))
                expo = jnp.exp(scores - jnp.max(scores, axis=-1, keepdims=True)).astype(BF)
                results.append(dot(expo, jnp.where(own_k, values, one)))
            top = jnp.where(left_q, results[0], results[1])
            total = pltpu.roll(jnp.where(left_q, results[1], results[0]), HD, 1)
            attended = (top / total).astype(BF)
            att[step, 0, :, columns] = attended[:NP]
            att[step, 1, :, columns] = attended[NP:]
        remote(att.at[step, 1 - core], attx.at[step], asem.at[step], to_core).start()
        pltpu.make_async_copy(attx.at[step], attx.at[step], asem.at[step, 1]).wait()
        crossed = dot(att[step, core], wo_ref[...], ((1,), (1,)))
        crossed = (crossed + dot(attx[step], wox[...], ((1,), (1,)))).astype(BF)
        if step == 0:
            yb[...] = interleave(crossed)
            remote(yb, yx, bsem, to_view).start()
        else:
            s3[:, view] = interleave(crossed)
    pltpu.make_async_copy(yx, yx, bsem.at[1]).wait()
    s3[:, 1 - view] = yx[...]

    scatter(s3, r_ref, p3)
    r_ref[me] = s3[me]
    landed(r_ref, p3.at[1])
    total = dot(spread[0], r_ref[:, 0].reshape(2 * NP, HALF))
    total = total + dot(spread[1], r_ref[:, 1].reshape(2 * NP, HALF))
    s4[...] = (total / uses).astype(BF).reshape(NP, 2, HALF)
    scatter(s4, z_ref, p4)
    z_ref[me] = s4[me]
    landed(z_ref, p4.at[1])
    first, second = separate(z_ref[...])
    out_ref[:, :HALF] = (e_ref[:, :HALF].astype(F32) + first).astype(BF)
    out_ref[:, HALF:] = (e_ref[:, HALF:].astype(F32) + second).astype(BF)

    landed(s1, p1.at[0])
    for b in range(2):
        landed(s2.at[b], p2.at[b, 0])
        block = f_ref.at[b, mine]
        pltpu.make_async_copy(block, block, ysem.at[b, 0]).wait()
        pltpu.make_async_copy(block, block, csem.at[b, 0]).wait()
        pltpu.make_async_copy(block, block, fsem.at[b, 0]).wait()
        pltpu.make_async_copy(attx.at[b], attx.at[b], asem.at[b, 0]).wait()
    wox_wait.wait_send()
    pltpu.make_async_copy(yb, yb, bsem.at[0]).wait()
    landed(s3, p3.at[0])
    landed(s4, p4.at[0])


def body(enc_tokens, pairs, image_slot, embed_weight, norm_gains, cross_q, cross_kv, cross_out):
    cosine, sine = rope_tables()
    vmem = pl.BlockSpec(memory_space=pltpu.VMEM)
    message = (NP, 2, HALF)
    sems = pltpu.SemaphoreType.DMA
    out = pl.pallas_call(
        kernel,
        out_shape=jax.ShapeDtypeStruct((NP, DD), BF),
        in_specs=[vmem] * 10,
        out_specs=vmem,
        scratch_shapes=[
            pltpu.VMEM((NP, DD), BF),
            pltpu.VMEM(message, BF),
            pltpu.VMEM(message, BF),
            pltpu.VMEM((2,) + message, BF),
            pltpu.VMEM((2,) + message, BF),
            pltpu.VMEM((2, 4, NP, DD), BF),
            pltpu.VMEM((DD, HALF), BF),
            pltpu.VMEM((DD, HALF), BF),
            pltpu.VMEM((DD, HALF), BF),
            pltpu.VMEM((3, TOK, HALF), BF),
            pltpu.VMEM((2, 2, NP, HALF), BF),
            pltpu.VMEM((2, NP, HALF), BF),
            pltpu.VMEM(message, BF),
            pltpu.VMEM(message, BF),
            pltpu.VMEM((NP, 2, 2, HALF), BF),
            pltpu.VMEM((NP, 2, 2, HALF), BF),
            pltpu.VMEM(message, BF),
            pltpu.VMEM(message, BF),
            sems,
            sems((2,)),
            sems((2,)),
            sems((2, 2)),
            sems((2, 2)),
            sems((2, 2)),
            sems((2, 2)),
            sems((2, 2)),
            sems((2,)),
            sems((2,)),
            sems((2,)),
        ],
        compiler_params=pltpu.CompilerParams(
            collective_id=0, has_side_effects=True, vmem_limit_bytes=56 << 20
        ),
        name="cross_block",
    )(
        enc_tokens[0],
        pairs,
        image_slot.reshape(1, NP),
        embed_weight,
        norm_gains[0],
        cross_q[0],
        cross_kv[0],
        cross_out[0],
        cosine,
        sine,
    )
    return out[None]


def solution(mesh):
    placed = (
        P("pair", ("view", "head"), None),
        P(),
        P(),
        P(),
        P("view", None, None),
        P("view", None, "head"),
        P("view", None, None, "head"),
        P("view", None, "head"),
    )
    return jax.shard_map(
        body,
        mesh=mesh,
        in_specs=placed,
        out_specs=P("pair", ("view", "head"), None),
        check_vma=False,
    )
```

time: 347 us -> 116 us (0.33)
  waiting for transfers between devices: 163 us -> 0 us
  Pallas kernels: 0 us -> 113 us
  blocking collectives: 71.2 us -> 0 us
  starting transfers between devices: 38.1 us -> 0 us
  matrix products: 28 us -> 0 us
  local copies, waits for them, and re-layouts: 17.8 us -> 3.03 us
  between operations: 13.8 us -> 0.01 us
  other arithmetic: 12.6 us -> 0 us
    pallas_call x0 -> x1, Pallas kernels: none -> 113 us  [body(): pl.pallas_call(kernel, out_shape=jax.ShapeDtypeStruct((NP, DD), BF), in_s...]
    all_to_all x2 -> x0, waiting for transfers between devices: 87.3 us -> none  [the longest x1 69 us: body(): lax.all_to_all(stacked, 'pair', split_axis=1, concat_axis=1, tiled=True)]
    all_to_all x2 -> x0, blocking collectives: 71.2 us -> none  [the longest x1 36.7 us: body(): lax.all_to_all(outgoing, 'pair', split_axis=1, concat_axis=1, tiled=True)]
    reduce_scatter x1 -> x0, waiting for transfers between devices: 50.2 us -> none  [body(): lax.psum_scatter(summed, ('view', 'head'), scatter_dimension=0, tiled=True)]
    all_to_all x2 -> x0, starting transfers between devices: 38 us -> none  [the longest x1 21.3 us: body(): lax.all_to_all(enc_tokens, 'pair', split_axis=1, concat_axis=0, tiled=True)]
    dot_general x17 -> x0, matrix products: 28 us -> none  [the longest x6 11 us: one_head(): jnp.dot(weights, value_block, preferred_element_type=jnp.float32)]
    all_gather x1 -> x0, waiting for transfers between devices: 25.3 us -> none  [body(): lax.all_gather(own_quarter, ('view', 'head'), axis=1, tiled=True)]
    unnamed x2 -> x0, other arithmetic: 4.01 us -> none
  transfers between devices with their start and end apart: 4 -> 0, of which waited for: 4 -> 0; matrix products, arithmetic and copies ran while one was open for 1% -> 0% of each run, Pallas kernels for 0% -> 0%
where the time goes in v1:
time: 116 us
  Pallas kernels  113 us (97%)
  local copies, waits for them, and re-layouts  3.03 us (3%)
    pallas_call x1, Pallas kernels, body(): pl.pallas_call(kernel, out_shape=jax.ShapeDtypeStruct((NP, DD), BF), in_s...  113 us
    unnamed x2, local copies, waits for them, and re-layouts  3.03 us

profile of v1, /device:TPU:1, one launch (start us, length us, event | category | flops | bytes accessed | tf_op | source)
XLA Modules:
  0.0 116.0 jit_solution(7310378117387780621)
XLA Ops:
  0.0 1.4 %copy.11.pairs_ref = s32[128,2]{1,0:T(8,128)} copy(s32[128,2]{0,1:T(2,128)} %param.11) | data formatting | bytes 2048 | tf_op args[1]
  1.4 112.9 %cross_block.1 = bf16[128,768]{1,0:T(8,128)(2,1)} custom-call(bf16[128,1024]{1,0:T(8,128)(2,1)} %bitcast.11, s32[128,2]{1,0:T(8,128)} %copy.11.pairs_ref, s32[1,128]{1,0:T(1,128)} %bitcast.13, bf16[1024,768]{1,0:T(8,128)(2,1)} %emb_ref.1, f32[2,768]{1,0:T(2,128)} %bitcast.12, bf16[768,384]{1,0:T(8,128)(2,1)} %bitcast.9, bf16[768,2,384]{2,1,0:T(2,128)(2,1)} %bitcast.7, ...), custom_call_target="tpu_custom_call" | custom-call | tf_op jit(solution)/shard_map/cross_block/pallas_call | solution.py:245
  114.3 1.6 %copy.13 = bf16[1,128,768]{2,1,0:T(8,128)(2,1)} copy(bf16[1,128,768]{2,1,0:T(8,128)(2,1)} %bitcast.8) | data formatting | bytes 393216

commit v2 on v1

v2 whole, which is shorter than its diff:
```python
import jax
import jax.numpy as jnp
import numpy as np
from jax import lax
from jax.experimental import pallas as pl
from jax.experimental.pallas import tpu as pltpu
from jax.sharding import PartitionSpec as P

HD = 64
GRIDW = 32
TOK = 512
DD = 768
HALF = 384
NP = 128
BF = jnp.bfloat16
F32 = jnp.float32
MESH = pl.DeviceIdType.MESH
THROTTLE1 = False
THROTTLE2 = True
THROTTLE3 = True


def rope_tables():
    lane = np.arange(128)
    token = np.arange(TOK)
    place = np.where(
        ((lane % HD) // 32)[None, :] == 0, (token // GRIDW)[:, None], (token % GRIDW)[:, None]
    ).astype(np.float64)
    frequency = 100.0 ** (-2.0 * (lane % 16) / 32.0)
    angle = place * frequency[None, :]
    sign = np.where((lane % 32) < 16, -1.0, 1.0)
    return np.cos(angle).astype(np.float32), (np.sin(angle) * sign[None, :]).astype(np.float32)


def iota(shape, dim):
    return lax.broadcasted_iota(jnp.int32, shape, dim)


def onehot(mask):
    return jnp.where(mask, 1.0, 0.0).astype(BF)


def dot(a, b, dims=((1,), (0,))):
    return lax.dot_general(a, b, (dims, ((), ())), preferred_element_type=F32)


def kernel(
    x_hbm, pairs_ref, slot_ref, emb_hbm, gain_ref, wq_hbm, wkv_hbm, wo_hbm, cos_hbm, sin_hbm,
    e_ref, avg_ref,
    x_ref, emb_ref, wq_ref, wkv_ref, wo_ref, cos_ref, sin_ref,
    s1, h_ref, s2, t_ref, f_ref, wk, wv, wox, qkv, att, attx, s3, r_ref, s4, z_ref,
    in_sem, wo_sem, p1, p2, ysem, csem, fsem, asem, p3, p4,
):
    me = lax.axis_index("pair")
    view = lax.axis_index("view")
    core = lax.axis_index("head")
    mine = view * 2 + core
    half_me = me // 2
    odd_me = me - 2 * half_me
    to_core = {"head": 1 - core}
    to_view = {"view": 1 - view}

    def remote(src, dst, sent, got, where):
        return pltpu.make_async_remote_copy(
            src, dst, sent, got, device_id=where, device_id_type=MESH
        )

    def arrive(buf, sem):
        pltpu.make_async_copy(buf, buf, sem).wait()

    def landed(buf, sem, count=NP - 1):
        arrive(buf.at[pl.ds(0, count)], sem)

    loads = [
        pltpu.make_async_copy(src, dst, in_sem.at[i])
        for i, (src, dst) in enumerate(
            (
                (x_hbm, x_ref),
                (emb_hbm, emb_ref),
                (wo_hbm, wo_ref),
                (wkv_hbm, wkv_ref),
                (wq_hbm, wq_ref),
                (cos_hbm, cos_ref),
                (sin_hbm, sin_ref),
            )
        )
    ]
    for load in loads:
        load.start()

    barrier = pltpu.get_barrier_semaphore()

    def greet(k, carry):
        pl.semaphore_signal(
            barrier, inc=1, device_id={"pair": lax.rem(me + k, NP)}, device_id_type=MESH
        )
        return carry

    lax.fori_loop(1, NP, greet, 0)
    pl.semaphore_signal(barrier, inc=1, device_id=to_core, device_id_type=MESH)
    pl.semaphore_signal(barrier, inc=1, device_id=to_view, device_id_type=MESH)

    def scatter(src, dst, sent, got, first=1, last=NP):
        def send(k, carry):
            peer = lax.rem(me + k, NP)
            remote(src.at[peer], dst, sent, got, {"pair": peer}).start()
            return carry

        lax.fori_loop(first, last, send, 0)

    def scatter_half(src, dst, sent, got, parity, where=None):
        def send(i, carry):
            peer = 2 * lax.rem(half_me + i, NP // 2) + parity
            target = {"pair": peer} if where is None else {"pair": peer, **where}
            copy = remote(src.at[peer], dst, sent, got, target)
            if where is None:
                pl.when(peer != me)(copy.start)
            else:
                copy.start()
            return carry

        lax.fori_loop(0, NP // 2, send, 0)

    def half_left(buf, sem, parity):
        @pl.when(odd_me == parity)
        def _():
            landed(buf, sem, NP // 2 - 1)

        @pl.when(odd_me != parity)
        def _():
            landed(buf, sem, NP // 2)

    weave = [onehot(iota((2 * NP, NP), 0) == 2 * iota((2 * NP, NP), 1) + f) for f in range(2)]
    part = [onehot(iota((NP, 2 * NP), 1) == 2 * iota((NP, 2 * NP), 0) + f) for f in range(2)]

    def interleave(rows):
        both = dot(weave[0], rows[:, :HALF]) + dot(weave[1], rows[:, HALF:])
        return both.astype(BF).reshape(NP, 2, HALF)

    def separate(rows):
        flat = rows.reshape(2 * NP, HALF)
        return dot(part[0], flat).astype(BF), dot(part[1], flat).astype(BF)

    loads[0].wait()
    loads[1].wait()
    embedded = dot(x_ref[...], emb_ref[...]).astype(BF)
    e_ref[...] = embedded
    s1[...] = interleave(embedded)
    pl.semaphore_wait(barrier, NP + 1)
    scatter_half(s1, h_ref.at[me], p1.at[0], p1.at[2], 0)
    if not THROTTLE1:
        scatter_half(s1, h_ref.at[me], p1.at[1], p1.at[2], 1)
    h_ref[me] = s1[me]
    loads[2].wait()
    wo_copy = remote(wo_ref, wox, wo_sem.at[0], wo_sem.at[1], to_core)
    wo_copy.start()
    if THROTTLE1:
        half_left(s1, p1.at[0], 0)
        scatter_half(s1, h_ref.at[me], p1.at[1], p1.at[2], 1)

    pair_col = dot(
        onehot(iota((2 * NP, NP), 0) // 2 == iota((2 * NP, NP), 1)),
        pairs_ref[...].astype(BF),
        ((1,), (1,)),
    )
    slot_rows = onehot(iota((2 * NP, NP), 0) // 2 == slot_ref[...])
    same = (iota((2 * NP, 2 * NP), 0) - iota((2 * NP, 2 * NP), 1)) % 2 == 0
    pick, spread = [], []
    for b in range(2):
        image = onehot(iota((2 * NP, NP), 1) == pair_col[:, b : b + 1].astype(jnp.int32))
        pick.append(jnp.where(same, dot(image, slot_rows, ((1,), (1,))), 0.0).astype(BF))
        spread.append(jnp.where(same, dot(slot_rows, image, ((1,), (1,))), 0.0).astype(BF))
    uses = jnp.sum(spread[0].astype(F32) + spread[1].astype(F32), axis=1, keepdims=True)

    loads[3].wait()
    for block in range(DD // NP):
        rows = slice(block * NP, (block + 1) * NP)
        wk[rows, :], wv[rows, :] = separate(wkv_ref[rows])
    for load in loads[4:]:
        load.wait()

    landed(h_ref, p1.at[2])
    held = h_ref[...].reshape(2 * NP, HALF)
    for b in range(2):
        s2[b] = dot(pick[b], held).astype(BF).reshape(NP, 2, HALF)
        t_ref[b, me] = s2[b, me]
        for part_no, (first, last) in enumerate(((1, 65), (65, NP))):
            if b and THROTTLE2:
                landed(s2.at[0], p2.at[0, part_no], last - first)
            scatter(s2.at[b], t_ref.at[b, me], p2.at[b, part_no], p2.at[b, 2], first, last)

    def normalize(rows, gain):
        rows = rows.astype(F32)
        centered = rows - jnp.mean(rows, axis=-1, keepdims=True)
        variance = jnp.mean(centered * centered, axis=-1, keepdims=True)
        return (centered * lax.rsqrt(variance + 1e-06) * gain).astype(BF)

    low16 = iota((NP, 128), 1) % 32 < 16

    def rotate(rows, cosine, sine, scale):
        parts = []
        for block in range(HALF // 128):
            u = rows[:, block * 128 : (block + 1) * 128]
            swapped = jnp.where(low16, pltpu.roll(u, 112, 1), pltpu.roll(u, 16, 1))
            parts.append((u * cosine + swapped * sine).astype(BF) * scale)
        return jnp.concatenate(parts, axis=1)

    def image_step(b, carry):
        landed(t_ref.at[b], p2.at[b, 2])
        f_ref[b, mine, :, :HALF], f_ref[b, mine, :, HALF:] = separate(t_ref[b])
        for piece in range(2):
            block = f_ref.at[b, mine, pl.ds(piece * (NP // 2), NP // 2)]
            remote(block, block, ysem.at[b, piece, 0], ysem.at[b, piece, 1], to_view).start()
        block = f_ref.at[b, mine]
        remote(block, block, csem.at[b, 0], csem.at[b, 1], to_core).start()
        there = (1 - view) * 2 + core

        def quarter_step(k, carry):
            quarter = 2 * lax.rem(view + k // 2, 2) + lax.rem(core + k, 2)

            @pl.when(k == 1)
            def _():
                arrive(f_ref.at[b, mine], csem.at[b, 1])

            @pl.when(k == 2)
            def _():
                for piece in range(2):
                    block = f_ref.at[b, there, pl.ds(piece * (NP // 2), NP // 2)]
                    arrive(block, ysem.at[b, piece, 1])
                    remote(
                        block, block, fsem.at[b, piece, 0], fsem.at[b, piece, 1], to_core
                    ).start()

            @pl.when(k == 3)
            def _():
                for piece in range(2):
                    block = f_ref.at[b, there, pl.ds(piece * (NP // 2), NP // 2)]
                    arrive(block, fsem.at[b, piece, 1])

            tokens = f_ref[b, quarter]
            rows = pl.ds(pl.multiple_of(quarter * NP, NP), NP)
            cosine, sine = cos_ref[rows, :], sin_ref[rows, :]

            @pl.when(view == b)
            def _():
                query_in = normalize(tokens, gain_ref[0:1, :])
                qkv[0, rows, :] = rotate(dot(query_in, wq_ref[...]), cosine, sine, BF(HD**-0.5))

            @pl.when(view != b)
            def _():
                key_in = normalize(tokens, gain_ref[1:2, :])
                qkv[1, rows, :] = rotate(dot(key_in, wk[...]), cosine, sine, BF(1.0))
                qkv[2, rows, :] = dot(key_in, wv[...]).astype(BF)

            return carry

        return lax.fori_loop(0, 4, quarter_step, carry)

    lax.fori_loop(0, 2, image_step, 0)
    wo_copy.wait_recv()

    left_q = iota((2 * NP, 128), 1) < HD
    left_k = iota((TOK, 128), 1) < HD
    one = jnp.ones((), BF)
    zero = jnp.zeros((), BF)

    def attend(step, block):
        half = 1 - view if step == 0 else view
        rows = pl.ds(pl.multiple_of(half * 2 * NP, 2 * NP), 2 * NP)
        columns = slice(block * 128, (block + 1) * 128)
        queries = qkv[0, rows, columns]
        keys = qkv[1, :, columns]
        values = qkv[2, :, columns]
        results = []
        for side in range(2):
            own_q = left_q if side == 0 else jnp.logical_not(left_q)
            own_k = left_k if side == 0 else jnp.logical_not(left_k)
            scores = dot(jnp.where(own_q, queries, zero), keys, ((1,), (1,)))
            expo = jnp.exp(scores - jnp.max(scores, axis=-1, keepdims=True)).astype(BF)
            results.append(dot(expo, jnp.where(own_k, values, one)))
        top = jnp.where(left_q, results[0], results[1])
        total = pltpu.roll(jnp.where(left_q, results[1], results[0]), HD, 1)
        attended = (top / total).astype(BF)
        att[step, 0, :, columns] = attended[:NP]
        att[step, 1, :, columns] = attended[NP:]

    def swap_cores(step):
        remote(
            att.at[step, 1 - core], attx.at[step], asem.at[step, 0], asem.at[step, 1], to_core
        ).start()

    def finish(step):
        arrive(attx.at[step], asem.at[step, 1])
        crossed = dot(att[step, core], wo_ref[...], ((1,), (1,)))
        crossed = (crossed + dot(attx[step], wox[...], ((1,), (1,)))).astype(BF)
        s3[step] = interleave(crossed)

    def send_results(step, parity):
        scatter_half(
            s3.at[step], r_ref.at[view, me], p3.at[step, parity], p3.at[step, 2], parity,
            to_view if step == 0 else None,
        )

    for block in range(3):
        attend(0, block)
    swap_cores(0)
    attend(1, 0)
    finish(0)
    send_results(0, 0)
    attend(1, 1)
    attend(1, 2)
    swap_cores(1)
    finish(1)
    send_results(1, 0)
    r_ref[view, me] = s3[1, me]
    if THROTTLE3:
        landed(s3.at[0], p3.at[0, 0], NP // 2)
    send_results(0, 1)
    if THROTTLE3:
        half_left(s3.at[1], p3.at[1, 0], 0)
    send_results(1, 1)

    arrive(r_ref.at[0], p3.at[0, 2])
    landed(r_ref.at[0], p3.at[1, 2])
    total = dot(spread[0], r_ref[0].reshape(2 * NP, HALF))
    total = total + dot(spread[1], r_ref[1].reshape(2 * NP, HALF))
    s4[...] = (total / uses).astype(BF).reshape(NP, 2, HALF)
    scatter(s4, z_ref.at[me], p4.at[0], p4.at[1])
    z_ref[me] = s4[me]
    landed(z_ref, p4.at[1])
    avg_ref[:, :HALF], avg_ref[:, HALF:] = separate(z_ref[...])

    if not THROTTLE1:
        half_left(s1, p1.at[0], 0)
    half_left(s1, p1.at[1], 1)
    wo_copy.wait_send()
    for b in range(2):
        if b or not THROTTLE2:
            landed(s2.at[b], p2.at[b, 0], 64)
            landed(s2.at[b], p2.at[b, 1], 63)
        arrive(f_ref.at[b, mine], csem.at[b, 0])
        for piece in range(2):
            block = f_ref.at[b, mine, pl.ds(piece * (NP // 2), NP // 2)]
            arrive(block, ysem.at[b, piece, 0])
            arrive(block, fsem.at[b, piece, 0])
        arrive(attx.at[b], asem.at[b, 0])
    if not THROTTLE3:
        landed(s3.at[0], p3.at[0, 0], NP // 2)
        half_left(s3.at[1], p3.at[1, 0], 0)
    landed(s3.at[0], p3.at[0, 1], NP // 2)
    half_left(s3.at[1], p3.at[1, 1], 1)
    landed(s4, p4.at[0])


def body(enc_tokens, pairs, image_slot, embed_weight, norm_gains, cross_q, cross_kv, cross_out):
    cosine, sine = rope_tables()
    vmem = pl.BlockSpec(memory_space=pltpu.VMEM)
    far = pl.BlockSpec(memory_space=pl.ANY)
    message = (NP, 2, HALF)
    sems = pltpu.SemaphoreType.DMA
    quarter = jax.ShapeDtypeStruct((NP, DD), BF)
    embedded, average = pl.pallas_call(
        kernel,
        out_shape=(quarter, quarter),
        in_specs=[far, vmem, vmem, far, vmem, far, far, far, far, far],
        out_specs=(vmem, vmem),
        scratch_shapes=[
            pltpu.VMEM((NP, 1024), BF),
            pltpu.VMEM((1024, DD), BF),
            pltpu.VMEM((DD, HALF), BF),
            pltpu.VMEM((DD, 2, HALF), BF),
            pltpu.VMEM((DD, HALF), BF),
            pltpu.VMEM((TOK, 128), F32),
            pltpu.VMEM((TOK, 128), F32),
            pltpu.VMEM(message, BF),
            pltpu.VMEM(message, BF),
            pltpu.VMEM((2,) + message, BF),
            pltpu.VMEM((2,) + message, BF),
            pltpu.VMEM((2, 4, NP, DD), BF),
            pltpu.VMEM((DD, HALF), BF),
            pltpu.VMEM((DD, HALF), BF),
            pltpu.VMEM((DD, HALF), BF),
            pltpu.VMEM((3, TOK, HALF), BF),
            pltpu.VMEM((2, 2, NP, HALF), BF),
            pltpu.VMEM((2, NP, HALF), BF),
            pltpu.VMEM((2,) + message, BF),
            pltpu.VMEM((2,) + message, BF),
            pltpu.VMEM(message, BF),
            pltpu.VMEM(message, BF),
            sems((7,)),
            sems((2,)),
            sems((3,)),
            sems((2, 3)),
            sems((2, 2, 2)),
            sems((2, 2)),
            sems((2, 2, 2)),
            sems((2, 2)),
            sems((2, 3)),
            sems((2,)),
        ],
        compiler_params=pltpu.CompilerParams(
            collective_id=0, has_side_effects=True, vmem_limit_bytes=56 << 20
        ),
        name="cross_block",
    )(
        enc_tokens[0],
        pairs.T,
        image_slot.reshape(1, NP),
        embed_weight,
        norm_gains[0],
        cross_q[0],
        cross_kv[0],
        cross_out[0],
        cosine,
        sine,
    )
    return (embedded.astype(F32) + average.astype(F32)).astype(BF)[None]


def solution(mesh):
    placed = (
        P("pair", ("view", "head"), None),
        P(),
        P(),
        P(),
        P("view", None, None),
        P("view", None, "head"),
        P("view", None, None, "head"),
        P("view", None, "head"),
    )
    return jax.shard_map(
        body,
        mesh=mesh,
        in_specs=placed,
        out_specs=P("pair", ("view", "head"), None),
        check_vma=False,
    )
```

time: 116 us -> 108 us (0.931); the launches traced: 116 us -> 107 us
  Pallas kernels: 113 us -> 105 us
  local copies, waits for them, and re-layouts: 3.03 us -> 0 us
  other arithmetic: 0 us -> 1.75 us
    pallas_call x1, Pallas kernels: 113 us -> 105 us  [body(): pl.pallas_call(kernel, out_shape=(quarter, quarter), in_specs=[far, vmem,...]
    unnamed x2 -> x0, local copies, waits for them, and re-layouts: 3.03 us -> none
    broadcast_in_dim x0 -> x1, other arithmetic: none -> 1.75 us  [body(): return (embedded.astype(F32) + average.astype(F32)).astype(BF)[None]]
where the time goes in v2:
time: 108 us; the launch traced here: 107 us
  Pallas kernels  105 us (97%)
  other arithmetic  1.75 us (2%)
    pallas_call x1, Pallas kernels, body(): pl.pallas_call(kernel, out_shape=(quarter, quarter), in_specs=[far, vmem,...  105 us

profile of v2, /device:TPU:1, one launch (start us, length us, event | category | flops | bytes accessed | tf_op | source)
XLA Modules:
  0.0 106.7 jit_solution(234411859632048327)
XLA Ops:
  0.0 104.9 %cross_block.1 = (bf16[128,768]{1,0:T(8,128)(2,1)}, bf16[128,768]{1,0:T(8,128)(2,1)}) custom-call(bf16[128,1024]{1,0:T(8,128)(2,1)} %bitcast.12, s32[2,128]{1,0:T(2,128)} %bitcast.14, s32[1,128]{1,0:T(1,128)} %bitcast.15, bf16[1024,768]{1,0:T(8,128)(2,1)} %emb_hbm.1, f32[2,768]{1,0:T(2,128)} %bitcast.13, bf16[768,384]{1,0:T(8,128)(2,1)} %bitcast.10, ...), custom_call_target="tpu_custom_call" | custom-call | tf_op jit(solution)/shard_map/cross_block/pallas_call | solution.py:362
  105.0 1.7 %fusion = bf16[1,128,768]{2,1,0:T(8,128)(2,1)} fusion(bf16[128,768]{1,0:T(8,128)(2,1)} %get-tuple-element.8, bf16[128,768]{1,0:T(8,128)(2,1)} %get-tuple-element.7), kind=kLoop, calls=%fused_computation.1 | loop fusion | flops 393216 | bytes 589824 | tf_op jit(solution)/shard_map/broadcast_in_dim | solution.py:417

commit v3 on v2

v3 whole, which is shorter than its diff:
```python
import jax
import jax.numpy as jnp
import numpy as np
from jax import lax
from jax.experimental import pallas as pl
from jax.experimental.pallas import tpu as pltpu
from jax.sharding import PartitionSpec as P

HD = 64
GRIDW = 32
TOK = 512
DD = 768
HALF = 384
NP = 128
BF = jnp.bfloat16
F32 = jnp.float32
MESH = pl.DeviceIdType.MESH
GROUPS = 4
GROUP = NP // GROUPS
CLASSES = 4


def rope_tables():
    lane = np.arange(128)
    token = np.arange(TOK)
    place = np.where(
        ((lane % HD) // 32)[None, :] == 0, (token // GRIDW)[:, None], (token % GRIDW)[:, None]
    ).astype(np.float64)
    frequency = 100.0 ** (-2.0 * (lane % 16) / 32.0)
    angle = place * frequency[None, :]
    sign = np.where((lane % 32) < 16, -1.0, 1.0)
    return np.cos(angle).astype(np.float32), (np.sin(angle) * sign[None, :]).astype(np.float32)


def iota(shape, dim):
    return lax.broadcasted_iota(jnp.int32, shape, dim)


def onehot(mask):
    return jnp.where(mask, 1.0, 0.0).astype(BF)


def dot(a, b, dims=((1,), (0,))):
    return lax.dot_general(a, b, (dims, ((), ())), preferred_element_type=F32)


def kernel(
    x_hbm, pairs_ref, slot_ref, emb_hbm, gain_ref, wq_hbm, wkv_hbm, wo_hbm, cos_hbm, sin_hbm,
    e_ref, avg_ref,
    x_ref, emb_ref, wq_ref, wkv_ref, wo_ref, cos_ref, sin_ref,
    s1, h_ref, s2, t_ref, wk, wv, wox, qkv, att, attx, s3, r_ref, s4, z_ref,
    in_sem, wo_sem, p1, p2_sent, p2_got, y_sent, y_got, c_sem, f_sem, asem, p3, p4,
):
    me = lax.axis_index("pair")
    view = lax.axis_index("view")
    core = lax.axis_index("head")
    to_core = {"head": 1 - core}
    to_view = {"view": 1 - view}

    def remote(src, dst, sent, got, where):
        return pltpu.make_async_remote_copy(
            src, dst, sent, got, device_id=where, device_id_type=MESH
        )

    def arrive(buf, sem):
        pltpu.make_async_copy(buf, buf, sem).wait()

    def landed(buf, sem, count=NP - 1):
        arrive(buf.at[pl.ds(0, count)], sem)

    loads = [
        pltpu.make_async_copy(src, dst, in_sem.at[i])
        for i, (src, dst) in enumerate(
            (
                (x_hbm, x_ref),
                (emb_hbm, emb_ref),
                (wo_hbm, wo_ref),
                (wkv_hbm, wkv_ref),
                (wq_hbm, wq_ref),
                (cos_hbm, cos_ref),
                (sin_hbm, sin_ref),
            )
        )
    ]
    for load in loads:
        load.start()

    barrier = pltpu.get_barrier_semaphore()

    def greet(k, carry):
        pl.semaphore_signal(
            barrier, inc=1, device_id={"pair": lax.rem(me + k, NP)}, device_id_type=MESH
        )
        return carry

    lax.fori_loop(1, NP, greet, 0)
    pl.semaphore_signal(barrier, inc=1, device_id=to_core, device_id_type=MESH)
    pl.semaphore_signal(barrier, inc=1, device_id=to_view, device_id_type=MESH)

    def scatter(src, dst, sent, got, first=1, last=NP, relative=False):
        def send(k, carry):
            peer = lax.rem(me + k, NP)
            place = k if relative else me
            remote(src.at[peer], dst.at[place], sent, got, {"pair": peer}).start()
            return carry

        lax.fori_loop(first, last, send, 0)

    def scatter_class(step, one):
        stride = NP // CLASSES

        def send(i, carry):
            peer = CLASSES * lax.rem(me // CLASSES + i, stride) + one
            target = {"pair": peer, "view": 1 - view if step == 0 else view}
            copy = remote(
                s3.at[step, peer], r_ref.at[view, me], p3.at[step, 0], p3.at[step, 1], target
            )
            if step == 0:
                copy.start()
            else:
                pl.when(peer != me)(copy.start)
            return carry

        lax.fori_loop(0, stride, send, 0)

    weave = [onehot(iota((2 * NP, NP), 0) == 2 * iota((2 * NP, NP), 1) + f) for f in range(2)]
    column, row = iota((NP, 2 * NP), 1), iota((NP, 2 * NP), 0)
    part = [onehot(column == 2 * row + f) for f in range(2)]
    turned = [onehot(column == 2 * lax.rem(me - row + NP, NP) + f) for f in range(2)]

    def interleave(rows):
        both = dot(weave[0], rows[:, :HALF]) + dot(weave[1], rows[:, HALF:])
        return both.astype(BF).reshape(NP, 2, HALF)

    def separate(rows, order):
        flat = rows.reshape(2 * NP, HALF)
        return dot(order[0], flat).astype(BF), dot(order[1], flat).astype(BF)

    loads[0].wait()
    loads[1].wait()
    embedded = dot(x_ref[...], emb_ref[...]).astype(BF)
    e_ref[...] = embedded
    s1[...] = interleave(embedded)
    pl.semaphore_wait(barrier, NP + 1)
    scatter(s1, h_ref, p1.at[0], p1.at[1])
    h_ref[me] = s1[me]
    loads[2].wait()
    wo_copy = remote(wo_ref, wox, wo_sem.at[0], wo_sem.at[1], to_core)
    wo_copy.start()

    pair_col = dot(
        onehot(iota((2 * NP, NP), 0) // 2 == iota((2 * NP, NP), 1)),
        pairs_ref[...].astype(BF),
        ((1,), (1,)),
    )
    slot_rows = onehot(iota((2 * NP, NP), 0) // 2 == slot_ref[...])
    same = (iota((2 * NP, 2 * NP), 0) - iota((2 * NP, 2 * NP), 1)) % 2 == 0
    pick, spread = [], []
    for b in range(2):
        image = onehot(iota((2 * NP, NP), 1) == pair_col[:, b : b + 1].astype(jnp.int32))
        pick.append(jnp.where(same, dot(image, slot_rows, ((1,), (1,))), 0.0).astype(BF))
        spread.append(jnp.where(same, dot(slot_rows, image, ((1,), (1,))), 0.0).astype(BF))
    uses = jnp.sum(spread[0].astype(F32) + spread[1].astype(F32), axis=1, keepdims=True)

    loads[3].wait()
    for block in range(DD // NP):
        rows = slice(block * NP, (block + 1) * NP)
        wk[rows, :], wv[rows, :] = separate(wkv_ref[rows], part)
    for load in loads[4:]:
        load.wait()

    landed(h_ref, p1.at[1])
    held = h_ref[...].reshape(2 * NP, HALF)
    for b in range(2):
        s2[b] = dot(pick[b], held).astype(BF).reshape(NP, 2, HALF)
        for g in range(GROUPS):
            scatter(
                s2.at[b], t_ref.at[b, 0], p2_sent.at[b], p2_got.at[b, g],
                max(g * GROUP, 1), (g + 1) * GROUP, relative=True,
            )
        t_ref[b, 0, 0] = s2[b, me]

    def across(n):
        b, g = divmod(n, GROUPS)
        place = pl.ds(g * GROUP, GROUP)
        new = pl.ds(max(g * GROUP, 1), GROUP if g else GROUP - 1)
        arrive(t_ref.at[b, 0, new], p2_got.at[b, g])
        block = t_ref.at[b, 0, place]
        remote(block, t_ref.at[b, 2, place], y_sent.at[b], y_got.at[b, g], to_view).start()
        remote(block, t_ref.at[b, 1, place], c_sem.at[b, 0], c_sem.at[b, 1], to_core).start()

    def onward(n):
        b, g = divmod(n, GROUPS)
        place = pl.ds(g * GROUP, GROUP)
        block = t_ref.at[b, 2, place]
        arrive(block, y_got.at[b, g])
        remote(block, t_ref.at[b, 3, place], f_sem.at[b, 0], f_sem.at[b, 1], to_core).start()

    for n in range(2 * GROUPS):
        across(n)
        if n >= 2:
            onward(n - 2)

    def normalize(rows, gain):
        rows = rows.astype(F32)
        centered = rows - jnp.mean(rows, axis=-1, keepdims=True)
        variance = jnp.mean(centered * centered, axis=-1, keepdims=True)
        return (centered * lax.rsqrt(variance + 1e-06) * gain).astype(BF)

    low16 = iota((NP, 128), 1) % 32 < 16

    def rotate(rows, cosine, sine, scale):
        parts = []
        for block in range(HALF // 128):
            u = rows[:, block * 128 : (block + 1) * 128]
            swapped = jnp.where(low16, pltpu.roll(u, 112, 1), pltpu.roll(u, 16, 1))
            parts.append((u * cosine + swapped * sine).astype(BF) * scale)
        return jnp.concatenate(parts, axis=1)

    def project(n, carry):
        b, kind = n // 4, n % 4
        quarter = 2 * lax.rem(view + kind // 2, 2) + lax.rem(core + kind, 2)

        @pl.when(n == 1)
        def _():
            onward(2 * GROUPS - 2)

        @pl.when(n == 4)
        def _():
            onward(2 * GROUPS - 1)

        @pl.when(kind == 1)
        def _():
            arrive(t_ref.at[b, 1], c_sem.at[b, 1])

        @pl.when(kind == 3)
        def _():
            arrive(t_ref.at[b, 3], f_sem.at[b, 1])

        tokens = jnp.concatenate(separate(t_ref[b, kind], turned), axis=1)
        rows = pl.ds(pl.multiple_of(quarter * NP, NP), NP)
        cosine, sine = cos_ref[rows, :], sin_ref[rows, :]

        @pl.when(view == b)
        def _():
            query_in = normalize(tokens, gain_ref[0:1, :])
            qkv[0, rows, :] = rotate(dot(query_in, wq_ref[...]), cosine, sine, BF(HD**-0.5))

        @pl.when(view != b)
        def _():
            key_in = normalize(tokens, gain_ref[1:2, :])
            qkv[1, rows, :] = rotate(dot(key_in, wk[...]), cosine, sine, BF(1.0))
            qkv[2, rows, :] = dot(key_in, wv[...]).astype(BF)

        return carry

    lax.fori_loop(0, 8, project, 0)
    wo_copy.wait_recv()

    left_q = iota((2 * NP, 128), 1) < HD
    left_k = iota((TOK, 128), 1) < HD
    one = jnp.ones((), BF)
    zero = jnp.zeros((), BF)

    def attend(step, block):
        half = 1 - view if step == 0 else view
        rows = pl.ds(pl.multiple_of(half * 2 * NP, 2 * NP), 2 * NP)
        columns = slice(block * 128, (block + 1) * 128)
        queries = qkv[0, rows, columns]
        keys = qkv[1, :, columns]
        values = qkv[2, :, columns]
        scores = []
        for side in range(2):
            own_q = left_q if side == 0 else jnp.logical_not(left_q)
            scores.append(dot(jnp.where(own_q, queries, zero), keys, ((1,), (1,))))
        expos = [
            jnp.exp(one_side - jnp.max(one_side, axis=-1, keepdims=True)).astype(BF)
            for one_side in scores
        ]
        results = [
            dot(expos[0], jnp.where(left_k, values, one)),
            dot(expos[1], jnp.where(left_k, one, values)),
        ]
        top = jnp.where(left_q, results[0], results[1])
        total = pltpu.roll(jnp.where(left_q, results[1], results[0]), HD, 1)
        attended = (top / total).astype(BF)
        att[step, 0, :, columns] = attended[:NP]
        att[step, 1, :, columns] = attended[NP:]

    def swap_cores(step):
        remote(
            att.at[step, 1 - core], attx.at[step], asem.at[step, 0], asem.at[step, 1], to_core
        ).start()

    def finish(step):
        arrive(attx.at[step], asem.at[step, 1])
        crossed = dot(att[step, core], wo_ref[...], ((1,), (1,)))
        crossed = (crossed + dot(attx[step], wox[...], ((1,), (1,)))).astype(BF)
        s3[step] = interleave(crossed)

    for block in range(3):
        attend(0, block)
    swap_cores(0)
    attend(1, 0)
    finish(0)
    for one in range(CLASSES // 2):
        scatter_class(0, one)
    attend(1, 1)
    attend(1, 2)
    swap_cores(1)
    finish(1)
    for one in range(CLASSES):
        if one >= CLASSES // 2:
            scatter_class(0, one)
        scatter_class(1, one)
    r_ref[view, me] = s3[1, me]

    arrive(r_ref.at[0], p3.at[0, 1])
    landed(r_ref.at[0], p3.at[1, 1])
    total = dot(spread[0], r_ref[0].reshape(2 * NP, HALF))
    total = total + dot(spread[1], r_ref[1].reshape(2 * NP, HALF))
    s4[...] = (total / uses).astype(BF).reshape(NP, 2, HALF)
    scatter(s4, z_ref, p4.at[0], p4.at[1])
    z_ref[me] = s4[me]
    landed(z_ref, p4.at[1])
    avg_ref[:, :HALF], avg_ref[:, HALF:] = separate(z_ref[...], part)

    landed(s1, p1.at[0])
    wo_copy.wait_send()
    for b in range(2):
        landed(s2.at[b], p2_sent.at[b])
        arrive(t_ref.at[b, 0], y_sent.at[b])
        arrive(t_ref.at[b, 0], c_sem.at[b, 0])
        arrive(t_ref.at[b, 2], f_sem.at[b, 0])
        arrive(attx.at[b], asem.at[b, 0])
    arrive(s3.at[0], p3.at[0, 0])
    landed(s3.at[1], p3.at[1, 0])
    landed(s4, p4.at[0])


def body(enc_tokens, pairs, image_slot, embed_weight, norm_gains, cross_q, cross_kv, cross_out):
    cosine, sine = rope_tables()
    vmem = pl.BlockSpec(memory_space=pltpu.VMEM)
    far = pl.BlockSpec(memory_space=pl.ANY)
    message = (NP, 2, HALF)
    sems = pltpu.SemaphoreType.DMA
    quarter = jax.ShapeDtypeStruct((NP, DD), BF)
    embedded, average = pl.pallas_call(
        kernel,
        out_shape=(quarter, quarter),
        in_specs=[far, vmem, vmem, far, vmem, far, far, far, far, far],
        out_specs=(vmem, vmem),
        scratch_shapes=[
            pltpu.VMEM((NP, 1024), BF),
            pltpu.VMEM((1024, DD), BF),
            pltpu.VMEM((DD, HALF), BF),
            pltpu.VMEM((DD, 2, HALF), BF),
            pltpu.VMEM((DD, HALF), BF),
            pltpu.VMEM((TOK, 128), F32),
            pltpu.VMEM((TOK, 128), F32),
            pltpu.VMEM(message, BF),
            pltpu.VMEM(message, BF),
            pltpu.VMEM((2,) + message, BF),
            pltpu.VMEM((2, 4) + message, BF),
            pltpu.VMEM((DD, HALF), BF),
            pltpu.VMEM((DD, HALF), BF),
            pltpu.VMEM((DD, HALF), BF),
            pltpu.VMEM((3, TOK, HALF), BF),
            pltpu.VMEM((2, 2, NP, HALF), BF),
            pltpu.VMEM((2, NP, HALF), BF),
            pltpu.VMEM((2,) + message, BF),
            pltpu.VMEM((2,) + message, BF),
            pltpu.VMEM(message, BF),
            pltpu.VMEM(message, BF),
            sems((7,)),
            sems((2,)),
            sems((2,)),
            sems((2,)),
            sems((2, GROUPS)),
            sems((2,)),
            sems((2, GROUPS)),
            sems((2, 2)),
            sems((2, 2)),
            sems((2, 2)),
            sems((2, 2)),
            sems((2,)),
        ],
        compiler_params=pltpu.CompilerParams(
            collective_id=0, has_side_effects=True, vmem_limit_bytes=56 << 20
        ),
        name="cross_block",
    )(
        enc_tokens[0],
        pairs.T,
        image_slot.reshape(1, NP),
        embed_weight,
        norm_gains[0],
        cross_q[0],
        cross_kv[0],
        cross_out[0],
        cosine,
        sine,
    )
    return (embedded.astype(F32) + average.astype(F32)).astype(BF)[None]


def solution(mesh):
    placed = (
        P("pair", ("view", "head"), None),
        P(),
        P(),
        P(),
        P("view", None, None),
        P("view", None, "head"),
        P("view", None, None, "head"),
        P("view", None, "head"),
    )
    return jax.shard_map(
        body,
        mesh=mesh,
        in_specs=placed,
        out_specs=P("pair", ("view", "head"), None),
        check_vma=False,
    )
```

time: 108 us -> 107 us (level)
  no operation moved by 1% of the time
where the time goes in v3:
time: 107 us
  Pallas kernels  105 us (98%)
  other arithmetic  1.75 us (2%)
    pallas_call x1, Pallas kernels, body(): pl.pallas_call(kernel, out_shape=(quarter, quarter), in_specs=[far, vmem,...  105 us

profile of v3, /device:TPU:1, one launch (start us, length us, event | category | flops | bytes accessed | tf_op | source)
XLA Modules:
  0.0 106.8 jit_solution(2667095591276820592)
XLA Ops:
  0.0 105.0 %cross_block.1 = (bf16[128,768]{1,0:T(8,128)(2,1)}, bf16[128,768]{1,0:T(8,128)(2,1)}) custom-call(bf16[128,1024]{1,0:T(8,128)(2,1)} %bitcast.12, s32[2,128]{1,0:T(2,128)} %bitcast.14, s32[1,128]{1,0:T(1,128)} %bitcast.15, bf16[1024,768]{1,0:T(8,128)(2,1)} %emb_hbm.1, f32[2,768]{1,0:T(2,128)} %bitcast.13, bf16[768,384]{1,0:T(8,128)(2,1)} %bitcast.10, ...), custom_call_target="tpu_custom_call" | custom-call | tf_op jit(solution)/shard_map/cross_block/pallas_call | solution.py:348
  105.0 1.7 %fusion = bf16[1,128,768]{2,1,0:T(8,128)(2,1)} fusion(bf16[128,768]{1,0:T(8,128)(2,1)} %get-tuple-element.8, bf16[128,768]{1,0:T(8,128)(2,1)} %get-tuple-element.7), kind=kLoop, calls=%fused_computation.1 | loop fusion | flops 393216 | bytes 589824 | tf_op jit(solution)/shard_map/broadcast_in_dim | solution.py:404

commit v4 on v3

--- a/solution.py
+++ b/solution.py
@@ -196,11 +196,6 @@
         arrive(block, y_got.at[b, g])
         remote(block, t_ref.at[b, 3, place], f_sem.at[b, 0], f_sem.at[b, 1], to_core).start()
 
-    for n in range(2 * GROUPS):
-        across(n)
-        if n >= 2:
-            onward(n - 2)
-
     def normalize(rows, gain):
         rows = rows.astype(F32)
         centered = rows - jnp.mean(rows, axis=-1, keepdims=True)
@@ -221,11 +216,7 @@
         b, kind = n // 4, n % 4
         quarter = 2 * lax.rem(view + kind // 2, 2) + lax.rem(core + kind, 2)
 
-        @pl.when(n == 1)
-        def _():
-            onward(2 * GROUPS - 2)
-
-        @pl.when(n == 4)
+        @pl.when(n == 5)
         def _():
             onward(2 * GROUPS - 1)
 
@@ -254,7 +245,14 @@
 
         return carry
 
-    lax.fori_loop(0, 8, project, 0)
+    for n in range(2 * GROUPS):
+        across(n)
+        if n >= 2:
+            onward(n - 2)
+        if 0 <= n - GROUPS < 3:
+            project(n - GROUPS, 0)
+    onward(2 * GROUPS - 2)
+    lax.fori_loop(3, 8, project, 0)
     wo_copy.wait_recv()
 
     left_q = iota((2 * NP, 128), 1) < HD

time: 107 us -> 105 us (0.981)
  Pallas kernels: 105 us -> 103 us
    pallas_call x1, Pallas kernels: 105 us -> 103 us  [body(): pl.pallas_call(kernel, out_shape=(quarter, quarter), in_specs=[far, vmem,...]
where the time goes in v4:
time: 105 us
  Pallas kernels  103 us (98%)
  other arithmetic  1.75 us (2%)
    pallas_call x1, Pallas kernels, body(): pl.pallas_call(kernel, out_shape=(quarter, quarter), in_specs=[far, vmem,...  103 us

profile of v4, /device:TPU:1, one launch (start us, length us, event | category | flops | bytes accessed | tf_op | source)
XLA Modules:
  0.0 105.1 jit_solution(7807210371526395303)
XLA Ops:
  0.0 103.3 %cross_block.1 = (bf16[128,768]{1,0:T(8,128)(2,1)}, bf16[128,768]{1,0:T(8,128)(2,1)}) custom-call(bf16[128,1024]{1,0:T(8,128)(2,1)} %bitcast.12, s32[2,128]{1,0:T(2,128)} %bitcast.14, s32[1,128]{1,0:T(1,128)} %bitcast.15, bf16[1024,768]{1,0:T(8,128)(2,1)} %emb_hbm.1, f32[2,768]{1,0:T(2,128)} %bitcast.13, bf16[768,384]{1,0:T(8,128)(2,1)} %bitcast.10, ...), custom_call_target="tpu_custom_call" | custom-call | tf_op jit(solution)/shard_map/cross_block/pallas_call | solution.py:346
  103.3 1.7 %fusion = bf16[1,128,768]{2,1,0:T(8,128)(2,1)} fusion(bf16[128,768]{1,0:T(8,128)(2,1)} %get-tuple-element.8, bf16[128,768]{1,0:T(8,128)(2,1)} %get-tuple-element.7), kind=kLoop, calls=%fused_computation.1 | loop fusion | flops 393216 | bytes 589824 | tf_op jit(solution)/shard_map/broadcast_in_dim | solution.py:402
